TPU v7x, 256 devices: a whole 4x4x8 slice. The times are simulated.
256 devices in a mesh: pipe: 4 (over z_lo, core), fsdp: 64 (over x, z_hi, y).
Axes of the slice: x: 4, y: 4, z: 8 (z_hi: 4, z_lo: 2; z = z_hi * 2 + z_lo), core: 2. Of those that a mesh axis runs over, the one named last changes fastest.
Arguments:
- tokens: int32 [2, 160], replicated, may hold values from 0 to 511
- embed: bfloat16 [512, 8192], P(None, 'fsdp'), may hold values from -60 to 60
- gain: bfloat16 [4, 8192], P('pipe', 'fsdp'), may hold values from 0.099609375 to 1.8984375
- w_in: bfloat16 [4, 3, 8192, 8192], P('pipe', None, None, 'fsdp'), may hold values from -0.0625 to 0.0625
- short_filter: float32 [4, 3, 7, 8192], P('pipe', None, None, 'fsdp'), may hold values from -2 to 2
- long_filter: float32 [4, 512, 128], P('pipe', 'fsdp'), may hold values from -0.5 to 0.5
- skip_bias: float32 [4, 8192], P('pipe', 'fsdp'), may hold values from -1 to 1
- w_out: bfloat16 [4, 8192, 8192], P('pipe', None, 'fsdp'), may hold values from -0.0625 to 0.0625
Outputs:
- hidden: bfloat16 [2, 160, 8192], P(None, 'pipe', 'fsdp')
All inputs are finite; a program needn't handle non-finite values.
Results may differ from a plain program's by a relative error of at most 0.035.
Values may be sent and summed in bfloat16 or wider, within the bound.
No kernel may reach another device: no remote copies, remote signals or barrier semaphores. Data moves between devices by JAX's collectives and lax.ppermute only.
A program may use at most 64 MiB of HBM per device.

v0:
```python
import jax
import jax.numpy as jnp
from jax import lax
from jax.sharding import PartitionSpec as P

D = 8192
GROUP = 16


def from_behind(block, axis, distance):
    devices = range(lax.axis_size(axis))
    route = [(i - distance, i) for i in devices if i - distance in devices]
    return lax.ppermute(block, axis, route)


def spread(value, axis, root):
    mine = lax.axis_index(axis) == root
    return lax.psum(jnp.where(mine, value, jnp.zeros_like(value)), axis)


def short_mix(projected, filters):
    width = filters.shape[1]
    seq_len = projected.shape[1]
    padded = jnp.pad(projected.astype(jnp.float32), ((0, 0), (width - 1, 0), (0, 0)))
    running = jnp.zeros(projected.shape, jnp.float32)
    for offset in range(width):
        window = padded[:, width - 1 - offset : width - 1 - offset + seq_len, :]
        running = running + filters[:, offset][:, None, :] * window
    return running


def long_mix(signal, kernels, group_size):
    seq_len = signal.shape[0]
    span = kernels.shape[1]
    count_filters = kernels.shape[0]
    positions = jnp.arange(seq_len, dtype=jnp.int32)
    lag_table = positions[:, None] - positions[None, :]
    inside = (lag_table >= 0) & (lag_table < span)
    lag_index = jnp.clip(lag_table, 0, span - 1)
    toeplitz = jnp.where(inside[None, :, :], kernels[:, lag_index], jnp.float32(0.0))
    grouped = signal.reshape(seq_len, count_filters, group_size)
    mixed = jnp.einsum("fts,sfg->tfg", toeplitz, grouped, precision=lax.Precision.HIGHEST)
    return mixed.reshape(seq_len, count_filters * group_size)


def body(tokens, embed, gain, w_in, short_filter, long_filter, skip_bias, w_out):
    segment_count = lax.axis_size("pipe")
    segment_index = lax.axis_index("pipe")
    batch_count = tokens.shape[0]
    seq_len = tokens.shape[1]
    local_width = embed.shape[1]
    in_weights = w_in[0]
    short_taps = short_filter[0]
    long_taps = long_filter[0]
    skip_row = skip_bias[0]
    out_weight = w_out[0]
    vocab_index = jnp.arange(embed.shape[0], dtype=jnp.int32)

    def layer_step(activation):
        widened = activation.astype(jnp.float32)
        squares = lax.psum(jnp.sum(widened * widened, axis=1), "fsdp")
        inverse_rms = lax.rsqrt(squares / D + 1e-06)[:, None]
        normalized = (widened * inverse_rms * gain.astype(jnp.float32)).astype(jnp.bfloat16)
        weight_rows = in_weights
        projected = jnp.einsum(
            "sk,jkc->jsc",
            lax.all_gather(normalized, "fsdp", axis=1, tiled=True),
            weight_rows,
            preferred_element_type=jnp.float32,
        )
        mixed = short_mix(projected.astype(jnp.bfloat16), short_taps)
        product = mixed[1] * mixed[2]
        carried = long_mix(product, long_taps, GROUP) + skip_row[None, :] * product
        gated = (mixed[0] * carried).astype(jnp.bfloat16)
        weight_rows = out_weight
        projected_out = jnp.dot(
            lax.all_gather(gated, "fsdp", axis=1, tiled=True),
            weight_rows,
            preferred_element_type=jnp.float32,
        )
        return (widened + projected_out).astype(jnp.bfloat16)

    def tick_body(tick_index, carry_state):
        previous, collected = carry_state
        incoming = from_behind(previous, "pipe", 1)
        micro_index = tick_index - segment_index
        chosen = jnp.clip(micro_index, 0, batch_count - 1)
        token_ids = lax.dynamic_index_in_dim(tokens, chosen, 0, keepdims=False)
        one_hot = (token_ids[:, None] == vocab_index[None, :]).astype(jnp.bfloat16)
        embedded = jnp.dot(one_hot, embed, preferred_element_type=jnp.float32).astype(jnp.bfloat16)
        activation = jnp.where(segment_index == 0, embedded, incoming)
        layer_out = layer_step(activation)
        store_flag = (
            (micro_index >= 0) & (micro_index < batch_count) & (segment_index == segment_count - 1)
        )
        updated = lax.dynamic_update_index_in_dim(collected, layer_out, chosen, 0)
        collected = jnp.where(store_flag, updated, collected)
        return (layer_out, collected)

    start_state = (
        jnp.zeros((seq_len, local_width), jnp.bfloat16),
        jnp.zeros((batch_count, seq_len, local_width), jnp.bfloat16),
    )
    final_state = lax.fori_loop(0, batch_count + segment_count - 1, tick_body, start_state)
    finished = spread(final_state[1], "pipe", segment_count - 1)
    row_share = seq_len // segment_count
    return lax.dynamic_slice_in_dim(finished, segment_index * row_share, row_share, 1)


def solution(mesh):
    return jax.shard_map(
        body,
        mesh=mesh,
        in_specs=(
            P(),
            P(None, "fsdp"),
            P("pipe", "fsdp"),
            P("pipe", None, None, "fsdp"),
            P("pipe", None, None, "fsdp"),
            P("pipe", "fsdp", None),
            P("pipe", "fsdp"),
            P("pipe", None, "fsdp"),
        ),
        out_specs=P(None, "pipe", "fsdp"),
        check_vma=False,
    )
```

profile of v0, /device:TPU:1, one launch (start us, length us, event | category | flops | bytes accessed | tf_op | source)
XLA Modules:
  0.0 2043.1 jit_solution(8263287136697875596)
XLA Ops:
  7.4 1.3 copy.20
  10.1 1982.0 %while.18 = (s32[]{:T(128)}, bf16[160,128]{1,0:T(8,128)(2,1)}, bf16[2,160,128]{2,1,0:T(8,128)(2,1)}, pred[]{:T(512)}, s32[]{:T(128)}, /*index=5*/s32[2,160]{1,0:...) while((s32[]{:T(128)}, bf16[160,128]{1,0:T(8,128)(2,1)}, ...), condition=%wide.region_3.4_spmd.clone, body=%wide.region_0.3_spmd.clone.sunk | while | flops 1404303872 | bytes 46493152 | solution.py:104
  10.1 4.9 collective-permute-start
  17.7 168.4 %psum.24 = f32[160]{0:T(256)S(1)} all-reduce(f32[160]{0:T(256)S(1)} %get-tuple-element.508), channel_id=1, replica_groups=mesh['pipe'=4,'fsdp'=64] {'fsdp'}, use_global_device_ids=true, to_apply=%region_2.2 | all-reduce | flops 160 | bytes 1280 | tf_op jit(solution)/shard_map/while/body/eval_jaxpr/psum | solution.py:61
  187.1 85.3 %gather_fusion = f32[25600,8]{1,0:T(8,128)} fusion(f32[8,128]{0,1:T(8,128)S(1)} %get-tuple-element.562, s32[25600]{0:T(1024)S(1)} %broadcast_clamp_fusion.2), kind=kCustom, calls=%fused_computation.clone.clone.1 | custom fusion | bytes 1740800 | tf_op jit(solution)/shard_map/while/body/eval_jaxpr/gather | solution.py:40
  272.4 8.8 copy.25
  281.8 1.4 slice_bitcast_fusion.9
  283.2 13.5 all-gather.3.cloned.1.call-done
  296.7 5.1 fusion.56
  303.4 1.6 copy.24
  305.1 2.8 fusion.58
  308.8 1.6 fusion.59
  310.4 96.4 %all-gather.5.cloned.1.call-done = bf16[160,8192]{1,0:T(8,128)(2,1)} async-done(((bf16[160,128]{1,0:T(8,128)(2,1)}), bf16[160,8192]{1,0:T(8,128)(2,1)}) %all-gather.5.cloned.1.call-update) | async-done | bytes 2621456 | tf_op jit(solution)/shard_map/while/body/eval_jaxpr/all_gather | solution.py:77
  406.9 3.2 fusion.60
  410.9 1.9 collective-permute-start
  415.4 166.0 %psum.24 = f32[160]{0:T(256)S(1)} all-reduce(f32[160]{0:T(256)S(1)} %get-tuple-element.508), channel_id=1, replica_groups=mesh['pipe'=4,'fsdp'=64] {'fsdp'}, use_global_device_ids=true, to_apply=%region_2.2 | all-reduce | flops 160 | bytes 1280 | tf_op jit(solution)/shard_map/while/body/eval_jaxpr/psum | solution.py:61
  582.4 85.3 %gather_fusion = f32[25600,8]{1,0:T(8,128)} fusion(f32[8,128]{0,1:T(8,128)S(1)} %get-tuple-element.562, s32[25600]{0:T(1024)S(1)} %broadcast_clamp_fusion.2), kind=kCustom, calls=%fused_computation.clone.clone.1 | custom fusion | bytes 1740800 | tf_op jit(solution)/shard_map/while/body/eval_jaxpr/gather | solution.py:40
  667.6 8.8 copy.25
  677.0 1.4 slice_bitcast_fusion.9
  678.5 13.8 all-gather.3.cloned.1.call-done
  692.3 5.1 fusion.56
  699.1 1.6 copy.24
  700.7 2.8 fusion.58
  704.5 1.6 fusion.59
  706.1 96.3 %all-gather.5.cloned.1.call-done = bf16[160,8192]{1,0:T(8,128)(2,1)} async-done(((bf16[160,128]{1,0:T(8,128)(2,1)}), bf16[160,8192]{1,0:T(8,128)(2,1)}) %all-gather.5.cloned.1.call-update) | async-done | bytes 2621456 | tf_op jit(solution)/shard_map/while/body/eval_jaxpr/all_gather | solution.py:77
  802.4 3.2 fusion.60
  806.4 1.9 collective-permute-start
  810.9 166.0 %psum.24 = f32[160]{0:T(256)S(1)} all-reduce(f32[160]{0:T(256)S(1)} %get-tuple-element.508), channel_id=1, replica_groups=mesh['pipe'=4,'fsdp'=64] {'fsdp'}, use_global_device_ids=true, to_apply=%region_2.2 | all-reduce | flops 160 | bytes 1280 | tf_op jit(solution)/shard_map/while/body/eval_jaxpr/psum | solution.py:61
  977.9 85.3 %gather_fusion = f32[25600,8]{1,0:T(8,128)} fusion(f32[8,128]{0,1:T(8,128)S(1)} %get-tuple-element.562, s32[25600]{0:T(1024)S(1)} %broadcast_clamp_fusion.2), kind=kCustom, calls=%fused_computation.clone.clone.1 | custom fusion | bytes 1740800 | tf_op jit(solution)/shard_map/while/body/eval_jaxpr/gather | solution.py:40
  1063.1 8.8 copy.25
  1072.6 1.4 slice_bitcast_fusion.9
  1074.0 13.8 all-gather.3.cloned.1.call-done
  1087.8 5.1 fusion.56
  1094.6 1.6 copy.24
  1096.2 2.8 fusion.58
  1100.0 1.6 fusion.59
  1101.6 96.3 %all-gather.5.cloned.1.call-done = bf16[160,8192]{1,0:T(8,128)(2,1)} async-done(((bf16[160,128]{1,0:T(8,128)(2,1)}), bf16[160,8192]{1,0:T(8,128)(2,1)}) %all-gather.5.cloned.1.call-update) | async-done | bytes 2621456 | tf_op jit(solution)/shard_map/while/body/eval_jaxpr/all_gather | solution.py:77
  1197.9 3.2 fusion.60
  1201.9 1.9 collective-permute-start
  1206.4 166.0 %psum.24 = f32[160]{0:T(256)S(1)} all-reduce(f32[160]{0:T(256)S(1)} %get-tuple-element.508), channel_id=1, replica_groups=mesh['pipe'=4,'fsdp'=64] {'fsdp'}, use_global_device_ids=true, to_apply=%region_2.2 | all-reduce | flops 160 | bytes 1280 | tf_op jit(solution)/shard_map/while/body/eval_jaxpr/psum | solution.py:61
  1373.4 85.3 %gather_fusion = f32[25600,8]{1,0:T(8,128)} fusion(f32[8,128]{0,1:T(8,128)S(1)} %get-tuple-element.562, s32[25600]{0:T(1024)S(1)} %broadcast_clamp_fusion.2), kind=kCustom, calls=%fused_computation.clone.clone.1 | custom fusion | bytes 1740800 | tf_op jit(solution)/shard_map/while/body/eval_jaxpr/gather | solution.py:40
  1458.6 8.8 copy.25
  1468.1 1.4 slice_bitcast_fusion.9
  1469.5 13.8 all-gather.3.cloned.1.call-done
  1483.3 5.1 fusion.56
  1490.1 1.6 copy.24
  1491.7 2.8 fusion.58
  1495.5 1.6 fusion.59
  1497.1 96.3 %all-gather.5.cloned.1.call-done = bf16[160,8192]{1,0:T(8,128)(2,1)} async-done(((bf16[160,128]{1,0:T(8,128)(2,1)}), bf16[160,8192]{1,0:T(8,128)(2,1)}) %all-gather.5.cloned.1.call-update) | async-done | bytes 2621456 | tf_op jit(solution)/shard_map/while/body/eval_jaxpr/all_gather | solution.py:77
  1593.4 3.2 fusion.60
  1597.4 1.9 collective-permute-start
  1601.9 166.0 %psum.24 = f32[160]{0:T(256)S(1)} all-reduce(f32[160]{0:T(256)S(1)} %get-tuple-element.508), channel_id=1, replica_groups=mesh['pipe'=4,'fsdp'=64] {'fsdp'}, use_global_device_ids=true, to_apply=%region_2.2 | all-reduce | flops 160 | bytes 1280 | tf_op jit(solution)/shard_map/while/body/eval_jaxpr/psum | solution.py:61
  1768.9 85.3 %gather_fusion = f32[25600,8]{1,0:T(8,128)} fusion(f32[8,128]{0,1:T(8,128)S(1)} %get-tuple-element.562, s32[25600]{0:T(1024)S(1)} %broadcast_clamp_fusion.2), kind=kCustom, calls=%fused_computation.clone.clone.1 | custom fusion | bytes 1740800 | tf_op jit(solution)/shard_map/while/body/eval_jaxpr/gather | solution.py:40
  1854.1 8.8 copy.25
  1863.6 1.4 slice_bitcast_fusion.9
  1865.0 13.8 all-gather.3.cloned.1.call-done
  1878.8 5.1 fusion.56
  1885.6 1.6 copy.24
  1887.2 2.8 fusion.58
  1891.0 1.6 fusion.59
  1892.6 96.3 %all-gather.5.cloned.1.call-done = bf16[160,8192]{1,0:T(8,128)(2,1)} async-done(((bf16[160,128]{1,0:T(8,128)(2,1)}), bf16[160,8192]{1,0:T(8,128)(2,1)}) %all-gather.5.cloned.1.call-update) | async-done | bytes 2621456 | tf_op jit(solution)/shard_map/while/body/eval_jaxpr/all_gather | solution.py:77
  1988.9 3.2 fusion.60
  1992.7 41.6 %all-reduce.3.cloned.1.call-done = bf16[2,160,128]{2,1,0:T(8,128)(2,1)} async-done(((bf16[2,160,128]{2,1,0:T(8,128)(2,1)}), bf16[2,160,128]{2,1,0:T(8,128)(2,1)}) %all-reduce.3.cloned.1.call-update) | async-done | bytes 81936 | tf_op jit(solution)/shard_map/psum | solution.py:18
  2034.4 1.3 constant_dynamic-slice_fusion.1
  (186 shorter events, 39.1 us)
Async XLA Ops:
  10.1 286.6 %all-gather.3.cloned.1.call-start = ((), (), s32[]{:S(2)}) async-start(), calls=%async_computation.1 | async-start | bytes 2662400 | tf_op jit(solution)/shard_map/while/body/eval_jaxpr/all_gather | solution.py:67
  10.1 6.3 collective-permute-start
  186.8 220.0 %all-gather.5.cloned.1.call-start = ((), (), s32[]{:S(2)}) async-start(), calls=%async_computation.2 | async-start | bytes 2662400 | tf_op jit(solution)/shard_map/while/body/eval_jaxpr/all_gather | solution.py:77
  296.7 5.2 copy-start.2
  296.7 5.2 copy-start.3
  296.7 5.2 copy-start.4
  296.7 5.2 copy-start.5
  296.7 5.2 copy-start.6
  296.7 5.2 copy-start.7
  296.7 5.2 copy-start.8
  301.8 105.1 %copy-start = (bf16[8192,128]{1,0:T(8,128)(2,1)S(1)}, bf16[8192,128]{1,0:T(8,128)(2,1)}, u32[]{:S(2)}) copy-start(bf16[8192,128]{1,0:T(8,128)(2,1)} %get-tuple-element.564) | copy-start | bytes 6291460 | tf_op jit(solution)/shard_map/while
  302.1 0.7 copy-start.1
  410.1 282.2 %all-gather.3.cloned.1.call-start = ((), (), s32[]{:S(2)}) async-start(), calls=%async_computation.1 | async-start | bytes 2662400 | tf_op jit(solution)/shard_map/while/body/eval_jaxpr/all_gather | solution.py:67
  410.9 3.3 collective-permute-start
  582.1 220.2 %all-gather.5.cloned.1.call-start = ((), (), s32[]{:S(2)}) async-start(), calls=%async_computation.2 | async-start | bytes 2662400 | tf_op jit(solution)/shard_map/while/body/eval_jaxpr/all_gather | solution.py:77
  692.3 5.2 copy-start.2
  692.3 5.2 copy-start.3
  692.3 5.2 copy-start.4
  692.3 5.2 copy-start.5
  692.3 5.2 copy-start.6
  692.3 5.2 copy-start.7
  692.3 5.2 copy-start.8
  697.4 104.9 %copy-start = (bf16[8192,128]{1,0:T(8,128)(2,1)S(1)}, bf16[8192,128]{1,0:T(8,128)(2,1)}, u32[]{:S(2)}) copy-start(bf16[8192,128]{1,0:T(8,128)(2,1)} %get-tuple-element.564) | copy-start | bytes 6291460 | tf_op jit(solution)/shard_map/while
  697.7 0.7 copy-start.1
  805.6 282.2 %all-gather.3.cloned.1.call-start = ((), (), s32[]{:S(2)}) async-start(), calls=%async_computation.1 | async-start | bytes 2662400 | tf_op jit(solution)/shard_map/while/body/eval_jaxpr/all_gather | solution.py:67
  806.4 3.3 collective-permute-start
  977.6 220.2 %all-gather.5.cloned.1.call-start = ((), (), s32[]{:S(2)}) async-start(), calls=%async_computation.2 | async-start | bytes 2662400 | tf_op jit(solution)/shard_map/while/body/eval_jaxpr/all_gather | solution.py:77
  1087.8 5.2 copy-start.2
  1087.8 5.2 copy-start.3
  1087.8 5.2 copy-start.4
  1087.8 5.2 copy-start.5
  1087.8 5.2 copy-start.6
  1087.8 5.2 copy-start.7
  1087.8 5.2 copy-start.8
  1093.0 104.9 %copy-start = (bf16[8192,128]{1,0:T(8,128)(2,1)S(1)}, bf16[8192,128]{1,0:T(8,128)(2,1)}, u32[]{:S(2)}) copy-start(bf16[8192,128]{1,0:T(8,128)(2,1)} %get-tuple-element.564) | copy-start | bytes 6291460 | tf_op jit(solution)/shard_map/while
  1093.2 0.7 copy-start.1
  1201.1 282.2 %all-gather.3.cloned.1.call-start = ((), (), s32[]{:S(2)}) async-start(), calls=%async_computation.1 | async-start | bytes 2662400 | tf_op jit(solution)/shard_map/while/body/eval_jaxpr/all_gather | solution.py:67
  1201.9 3.3 collective-permute-start
  1373.1 220.2 %all-gather.5.cloned.1.call-start = ((), (), s32[]{:S(2)}) async-start(), calls=%async_computation.2 | async-start | bytes 2662400 | tf_op jit(solution)/shard_map/while/body/eval_jaxpr/all_gather | solution.py:77
  1483.3 5.2 copy-start.2
  1483.3 5.2 copy-start.3
  1483.3 5.2 copy-start.4
  1483.3 5.2 copy-start.5
  1483.3 5.2 copy-start.6
  1483.3 5.2 copy-start.7
  1483.3 5.2 copy-start.8
  1488.4 104.9 %copy-start = (bf16[8192,128]{1,0:T(8,128)(2,1)S(1)}, bf16[8192,128]{1,0:T(8,128)(2,1)}, u32[]{:S(2)}) copy-start(bf16[8192,128]{1,0:T(8,128)(2,1)} %get-tuple-element.564) | copy-start | bytes 6291460 | tf_op jit(solution)/shard_map/while
  1488.7 0.7 copy-start.1
  1596.6 282.2 %all-gather.3.cloned.1.call-start = ((), (), s32[]{:S(2)}) async-start(), calls=%async_computation.1 | async-start | bytes 2662400 | tf_op jit(solution)/shard_map/while/body/eval_jaxpr/all_gather | solution.py:67
  1597.4 3.3 collective-permute-start
  1768.6 220.2 %all-gather.5.cloned.1.call-start = ((), (), s32[]{:S(2)}) async-start(), calls=%async_computation.2 | async-start | bytes 2662400 | tf_op jit(solution)/shard_map/while/body/eval_jaxpr/all_gather | solution.py:77
  1878.8 5.2 copy-start.2
  1878.8 5.2 copy-start.3
  1878.8 5.2 copy-start.4
  1878.8 5.2 copy-start.5
  1878.8 5.2 copy-start.6
  1878.8 5.2 copy-start.7
  1878.8 5.2 copy-start.8
  1883.9 104.9 %copy-start = (bf16[8192,128]{1,0:T(8,128)(2,1)S(1)}, bf16[8192,128]{1,0:T(8,128)(2,1)}, u32[]{:S(2)}) copy-start(bf16[8192,128]{1,0:T(8,128)(2,1)} %get-tuple-element.564) | copy-start | bytes 6291460 | tf_op jit(solution)/shard_map/while
  1884.2 0.7 copy-start.1
  1992.1 42.3 %all-reduce.3.cloned.1.call-start = ((), (), s32[]{:S(2)}) async-start(), calls=%async_computation | async-start | bytes 163840 | tf_op jit(solution)/shard_map/psum | solution.py:18
Sparse Core Ops, SparseCore 0:
  187.0 109.6 all-gather.2
  310.6 96.2 all-gather.4
  582.2 110.0 all-gather.2
  706.2 96.1 all-gather.4
  977.7 110.0 all-gather.2
  1101.7 96.1 all-gather.4
  1373.2 110.0 all-gather.2
  1497.2 96.1 all-gather.4
  1768.7 110.0 all-gather.2
  1892.7 96.1 all-gather.4
Sparse Core Ops, SparseCore 1:
  1995.2 39.2 all-reduce.2
where the time goes:
time: 2050 us; the launch traced here: 2040 us
  blocking collectives  832 us (41%)
  waiting for transfers between devices  592 us (29%)
  local copies, waits for them, and re-layouts  502 us (24%)
  matrix products  61.6 us (3%)
  other arithmetic  26.4 us (1%)
    psum x5, blocking collectives, layer_step(): squares = lax.psum(jnp.sum(widened * widened, axis=1), 'fsdp')  832 us
    all_gather x5, waiting for transfers between devices, layer_step(): lax.all_gather(gated, 'fsdp', axis=1, tiled=True)  482 us
    gather x10, local copies, waits for them, and re-layouts, long_mix(): kernels[:, lag_index]  470 us
    all_gather x5, waiting for transfers between devices, layer_step(): lax.all_gather(normalized, 'fsdp', axis=1, tiled=True)  68.8 us
    psum x1, waiting for transfers between devices, spread(): return lax.psum(jnp.where(mine, value, jnp.zeros_like(value)), axis)  41.6 us
  transfers between devices with their start and end apart: 16, of which 11 were waited for; matrix products, arithmetic and copies ran while one was open for 24% of the time, Pallas kernels for 0%

commit v1 on v0

--- a/solution.py
+++ b/solution.py
@@ -58,7 +58,9 @@
 
     def layer_step(activation):
         widened = activation.astype(jnp.float32)
-        squares = lax.psum(jnp.sum(widened * widened, axis=1), "fsdp")
+        part = jnp.sum(widened * widened, axis=1)
+        shards = lax.all_gather(part, "fsdp", axis=0, tiled=False)
+        squares = shards.sum(axis=0)
         inverse_rms = lax.rsqrt(squares / D + 1e-06)[:, None]
         normalized = (widened * inverse_rms * gain.astype(jnp.float32)).astype(jnp.bfloat16)
         weight_rows = in_weights

time: 2050 us -> 2970 us (1.45)
  blocking collectives: 832 us -> 1620 us
  waiting for transfers between devices: 592 us -> 721 us
    while x0 -> x5, blocking collectives: none -> 1620 us
    psum x5 -> x0, blocking collectives: 832 us -> none  [layer_step(): squares = lax.psum(jnp.sum(widened * widened, axis=1), 'fsdp')]
    all_gather x5, waiting for transfers between devices: 68.8 us -> 200 us  [layer_step(): lax.all_gather(normalized, 'fsdp', axis=1, tiled=True)]
  transfers between devices with their start and end apart: 16 -> 16, of which waited for: 11 -> 11; matrix products, arithmetic and copies ran while one was open for 24% -> 17% of each run, Pallas kernels for 0% -> 0%
where the time goes in v1:
time: 2970 us; the launch traced here: 2960 us
  blocking collectives  1620 us (55%)
  waiting for transfers between devices  721 us (24%)
  local copies, waits for them, and re-layouts  507 us (17%)
  matrix products  61.6 us (2%)
    while x5, blocking collectives  1620 us
    all_gather x5, waiting for transfers between devices, layer_step(): lax.all_gather(gated, 'fsdp', axis=1, tiled=True)  478 us
    gather x10, local copies, waits for them, and re-layouts, long_mix(): kernels[:, lag_index]  467 us
    all_gather x5, waiting for transfers between devices, layer_step(): lax.all_gather(normalized, 'fsdp', axis=1, tiled=True)  200 us
  transfers between devices with their start and end apart: 16, of which 11 were waited for; matrix products, arithmetic and copies ran while one was open for 17% of the time, Pallas kernels for 0%

profile of v1, /device:TPU:1, one launch (start us, length us, event | category | flops | bytes accessed | tf_op | source)
XLA Modules:
  0.0 2962.9 jit_solution(7122703678829182881)
XLA Ops:
  7.4 1.3 copy.25
  10.1 2901.7 %while.18 = (s32[]{:T(128)}, bf16[160,128]{1,0:T(8,128)(2,1)}, bf16[2,160,128]{2,1,0:T(8,128)(2,1)}, pred[]{:T(512)}, s32[]{:T(128)}, /*index=5*/s32[2,160]{1,0:...) while((s32[]{:T(128)}, bf16[160,128]{1,0:T(8,128)(2,1)}, ...), condition=%wide.region_3.4_spmd.clone, body=%wide.region_0.3_spmd.clone.sunk | while | flops 1404323968 | bytes 46739644 | solution.py:106
  10.1 4.9 collective-permute-start
  19.8 325.7 %all-reduce.4 = f32[10240]{0:T(1024)S(1)} all-reduce(f32[10240]{0:T(1024)S(1)} %dynamic-update-slice.9), channel_id=2, replica_groups=mesh['pipe'=4,'fsdp'=64] {'fsdp'}, use_global_device_ids=true, to_apply=%add.1 | all-reduce | flops 10240 | bytes 81920 | tf_op jit(solution)/shard_map/while
  346.6 84.6 %gather_fusion = f32[25600,8]{1,0:T(8,128)} fusion(f32[8,128]{0,1:T(8,128)S(1)} %get-tuple-element.570, s32[25600]{0:T(1024)S(1)} %broadcast_clamp_fusion.2), kind=kCustom, calls=%fused_computation.clone.clone.1 | custom fusion | bytes 1740800 | tf_op jit(solution)/shard_map/while/body/eval_jaxpr/gather | solution.py:40
  431.3 8.7 copy.30
  440.7 1.4 slice_bitcast_fusion.9
  442.1 39.4 %all-gather.4.cloned.1.call-done = bf16[160,8192]{1,0:T(8,128)(2,1)} async-done(((bf16[160,128]{1,0:T(8,128)(2,1)}), bf16[160,8192]{1,0:T(8,128)(2,1)}) %all-gather.4.cloned.1.call-update) | async-done | bytes 2621456 | tf_op jit(solution)/shard_map/while/body/eval_jaxpr/all_gather | solution.py:69
  481.5 5.1 fusion.56
  488.2 1.6 copy.29
  489.9 2.8 fusion.58
  493.6 1.6 fusion.59
  495.3 95.7 %all-gather.6.cloned.1.call-done = bf16[160,8192]{1,0:T(8,128)(2,1)} async-done(((bf16[160,128]{1,0:T(8,128)(2,1)}), bf16[160,8192]{1,0:T(8,128)(2,1)}) %all-gather.6.cloned.1.call-update) | async-done | bytes 2621456 | tf_op jit(solution)/shard_map/while/body/eval_jaxpr/all_gather | solution.py:79
  590.9 3.2 fusion.60
  594.9 1.9 collective-permute-start
  601.5 322.5 %all-reduce.4 = f32[10240]{0:T(1024)S(1)} all-reduce(f32[10240]{0:T(1024)S(1)} %dynamic-update-slice.9), channel_id=2, replica_groups=mesh['pipe'=4,'fsdp'=64] {'fsdp'}, use_global_device_ids=true, to_apply=%add.1 | all-reduce | flops 10240 | bytes 81920 | tf_op jit(solution)/shard_map/while
  925.2 84.6 %gather_fusion = f32[25600,8]{1,0:T(8,128)} fusion(f32[8,128]{0,1:T(8,128)S(1)} %get-tuple-element.570, s32[25600]{0:T(1024)S(1)} %broadcast_clamp_fusion.2), kind=kCustom, calls=%fused_computation.clone.clone.1 | custom fusion | bytes 1740800 | tf_op jit(solution)/shard_map/while/body/eval_jaxpr/gather | solution.py:40
  1009.8 8.7 copy.30
  1019.2 1.4 slice_bitcast_fusion.9
  1020.6 40.3 %all-gather.4.cloned.1.call-done = bf16[160,8192]{1,0:T(8,128)(2,1)} async-done(((bf16[160,128]{1,0:T(8,128)(2,1)}), bf16[160,8192]{1,0:T(8,128)(2,1)}) %all-gather.4.cloned.1.call-update) | async-done | bytes 2621456 | tf_op jit(solution)/shard_map/while/body/eval_jaxpr/all_gather | solution.py:69
  1060.9 5.1 fusion.56
  1067.6 1.6 copy.29
  1069.2 2.8 fusion.58
  1073.0 1.6 fusion.59
  1074.6 95.7 %all-gather.6.cloned.1.call-done = bf16[160,8192]{1,0:T(8,128)(2,1)} async-done(((bf16[160,128]{1,0:T(8,128)(2,1)}), bf16[160,8192]{1,0:T(8,128)(2,1)}) %all-gather.6.cloned.1.call-update) | async-done | bytes 2621456 | tf_op jit(solution)/shard_map/while/body/eval_jaxpr/all_gather | solution.py:79
  1170.3 3.2 fusion.60
  1174.3 1.9 collective-permute-start
  1180.9 322.5 %all-reduce.4 = f32[10240]{0:T(1024)S(1)} all-reduce(f32[10240]{0:T(1024)S(1)} %dynamic-update-slice.9), channel_id=2, replica_groups=mesh['pipe'=4,'fsdp'=64] {'fsdp'}, use_global_device_ids=true, to_apply=%add.1 | all-reduce | flops 10240 | bytes 81920 | tf_op jit(solution)/shard_map/while
  1504.6 84.6 %gather_fusion = f32[25600,8]{1,0:T(8,128)} fusion(f32[8,128]{0,1:T(8,128)S(1)} %get-tuple-element.570, s32[25600]{0:T(1024)S(1)} %broadcast_clamp_fusion.2), kind=kCustom, calls=%fused_computation.clone.clone.1 | custom fusion | bytes 1740800 | tf_op jit(solution)/shard_map/while/body/eval_jaxpr/gather | solution.py:40
  1589.2 8.7 copy.30
  1598.6 1.4 slice_bitcast_fusion.9
  1600.0 40.3 %all-gather.4.cloned.1.call-done = bf16[160,8192]{1,0:T(8,128)(2,1)} async-done(((bf16[160,128]{1,0:T(8,128)(2,1)}), bf16[160,8192]{1,0:T(8,128)(2,1)}) %all-gather.4.cloned.1.call-update) | async-done | bytes 2621456 | tf_op jit(solution)/shard_map/while/body/eval_jaxpr/all_gather | solution.py:69
  1640.3 5.1 fusion.56
  1647.1 1.6 copy.29
  1648.7 2.8 fusion.58
  1652.4 1.6 fusion.59
  1654.1 95.7 %all-gather.6.cloned.1.call-done = bf16[160,8192]{1,0:T(8,128)(2,1)} async-done(((bf16[160,128]{1,0:T(8,128)(2,1)}), bf16[160,8192]{1,0:T(8,128)(2,1)}) %all-gather.6.cloned.1.call-update) | async-done | bytes 2621456 | tf_op jit(solution)/shard_map/while/body/eval_jaxpr/all_gather | solution.py:79
  1749.8 3.2 fusion.60
  1753.8 1.9 collective-permute-start
  1760.4 322.5 %all-reduce.4 = f32[10240]{0:T(1024)S(1)} all-reduce(f32[10240]{0:T(1024)S(1)} %dynamic-update-slice.9), channel_id=2, replica_groups=mesh['pipe'=4,'fsdp'=64] {'fsdp'}, use_global_device_ids=true, to_apply=%add.1 | all-reduce | flops 10240 | bytes 81920 | tf_op jit(solution)/shard_map/while
  2084.0 84.6 %gather_fusion = f32[25600,8]{1,0:T(8,128)} fusion(f32[8,128]{0,1:T(8,128)S(1)} %get-tuple-element.570, s32[25600]{0:T(1024)S(1)} %broadcast_clamp_fusion.2), kind=kCustom, calls=%fused_computation.clone.clone.1 | custom fusion | bytes 1740800 | tf_op jit(solution)/shard_map/while/body/eval_jaxpr/gather | solution.py:40
  2168.7 8.7 copy.30
  2178.0 1.4 slice_bitcast_fusion.9
  2179.4 40.3 %all-gather.4.cloned.1.call-done = bf16[160,8192]{1,0:T(8,128)(2,1)} async-done(((bf16[160,128]{1,0:T(8,128)(2,1)}), bf16[160,8192]{1,0:T(8,128)(2,1)}) %all-gather.4.cloned.1.call-update) | async-done | bytes 2621456 | tf_op jit(solution)/shard_map/while/body/eval_jaxpr/all_gather | solution.py:69
  2219.7 5.1 fusion.56
  2226.5 1.6 copy.29
  2228.1 2.8 fusion.58
  2231.9 1.6 fusion.59
  2233.5 95.6 %all-gather.6.cloned.1.call-done = bf16[160,8192]{1,0:T(8,128)(2,1)} async-done(((bf16[160,128]{1,0:T(8,128)(2,1)}), bf16[160,8192]{1,0:T(8,128)(2,1)}) %all-gather.6.cloned.1.call-update) | async-done | bytes 2621456 | tf_op jit(solution)/shard_map/while/body/eval_jaxpr/all_gather | solution.py:79
  2329.2 3.2 fusion.60
  2333.2 1.9 collective-permute-start
  2339.8 322.5 %all-reduce.4 = f32[10240]{0:T(1024)S(1)} all-reduce(f32[10240]{0:T(1024)S(1)} %dynamic-update-slice.9), channel_id=2, replica_groups=mesh['pipe'=4,'fsdp'=64] {'fsdp'}, use_global_device_ids=true, to_apply=%add.1 | all-reduce | flops 10240 | bytes 81920 | tf_op jit(solution)/shard_map/while
  2663.5 84.6 %gather_fusion = f32[25600,8]{1,0:T(8,128)} fusion(f32[8,128]{0,1:T(8,128)S(1)} %get-tuple-element.570, s32[25600]{0:T(1024)S(1)} %broadcast_clamp_fusion.2), kind=kCustom, calls=%fused_computation.clone.clone.1 | custom fusion | bytes 1740800 | tf_op jit(solution)/shard_map/while/body/eval_jaxpr/gather | solution.py:40
  2748.1 8.7 copy.30
  2757.5 1.4 slice_bitcast_fusion.9
  2758.9 40.3 %all-gather.4.cloned.1.call-done = bf16[160,8192]{1,0:T(8,128)(2,1)} async-done(((bf16[160,128]{1,0:T(8,128)(2,1)}), bf16[160,8192]{1,0:T(8,128)(2,1)}) %all-gather.4.cloned.1.call-update) | async-done | bytes 2621456 | tf_op jit(solution)/shard_map/while/body/eval_jaxpr/all_gather | solution.py:69
  2799.2 5.1 fusion.56
  2805.9 1.6 copy.29
  2807.6 2.8 fusion.58
  2811.3 1.6 fusion.59
  2813.0 95.7 %all-gather.6.cloned.1.call-done = bf16[160,8192]{1,0:T(8,128)(2,1)} async-done(((bf16[160,128]{1,0:T(8,128)(2,1)}), bf16[160,8192]{1,0:T(8,128)(2,1)}) %all-gather.6.cloned.1.call-update) | async-done | bytes 2621456 | tf_op jit(solution)/shard_map/while/body/eval_jaxpr/all_gather | solution.py:79
  2908.6 3.2 fusion.60
  2912.5 41.6 %all-reduce.7.cloned.1.call-done = bf16[2,160,128]{2,1,0:T(8,128)(2,1)} async-done(((bf16[2,160,128]{2,1,0:T(8,128)(2,1)}), bf16[2,160,128]{2,1,0:T(8,128)(2,1)}) %all-reduce.7.cloned.1.call-update) | async-done | bytes 81936 | tf_op jit(solution)/shard_map/psum | solution.py:18
  2954.1 1.3 constant_dynamic-slice_fusion.1
  (211 shorter events, 47.4 us)
Async XLA Ops:
  10.1 471.3 %all-gather.4.cloned.1.call-start = ((), (), s32[]{:S(2)}) async-start(), calls=%async_computation.1 | async-start | bytes 2662400 | tf_op jit(solution)/shard_map/while/body/eval_jaxpr/all_gather | solution.py:69
  10.1 8.1 collective-permute-start
  346.4 244.5 %all-gather.6.cloned.1.call-start = ((), (), s32[]{:S(2)}) async-start(), calls=%async_computation.2 | async-start | bytes 2662400 | tf_op jit(solution)/shard_map/while/body/eval_jaxpr/all_gather | solution.py:79
  481.4 5.2 copy-start.2
  481.4 5.2 copy-start.3
  481.4 5.2 copy-start.4
  481.4 5.2 copy-start.5
  481.4 5.2 copy-start.6
  481.4 5.2 copy-start.7
  481.5 5.2 copy-start.8
  486.6 104.3 %copy-start = (bf16[8192,128]{1,0:T(8,128)(2,1)S(1)}, bf16[8192,128]{1,0:T(8,128)(2,1)}, u32[]{:S(2)}) copy-start(bf16[8192,128]{1,0:T(8,128)(2,1)} %get-tuple-element.572) | copy-start | bytes 6291460 | tf_op jit(solution)/shard_map/while
  486.9 0.7 copy-start.1
  594.1 466.7 %all-gather.4.cloned.1.call-start = ((), (), s32[]{:S(2)}) async-start(), calls=%async_computation.1 | async-start | bytes 2662400 | tf_op jit(solution)/shard_map/while/body/eval_jaxpr/all_gather | solution.py:69
  594.9 5.1 collective-permute-start
  924.9 245.4 %all-gather.6.cloned.1.call-start = ((), (), s32[]{:S(2)}) async-start(), calls=%async_computation.2 | async-start | bytes 2662400 | tf_op jit(solution)/shard_map/while/body/eval_jaxpr/all_gather | solution.py:79
  1060.8 5.2 copy-start.2
  1060.8 5.2 copy-start.3
  1060.8 5.2 copy-start.4
  1060.8 5.2 copy-start.5
  1060.8 5.2 copy-start.6
  1060.8 5.2 copy-start.7
  1060.8 5.2 copy-start.8
  1066.0 104.3 %copy-start = (bf16[8192,128]{1,0:T(8,128)(2,1)S(1)}, bf16[8192,128]{1,0:T(8,128)(2,1)}, u32[]{:S(2)}) copy-start(bf16[8192,128]{1,0:T(8,128)(2,1)} %get-tuple-element.572) | copy-start | bytes 6291460 | tf_op jit(solution)/shard_map/while
  1066.3 0.7 copy-start.1
  1173.5 466.8 %all-gather.4.cloned.1.call-start = ((), (), s32[]{:S(2)}) async-start(), calls=%async_computation.1 | async-start | bytes 2662400 | tf_op jit(solution)/shard_map/while/body/eval_jaxpr/all_gather | solution.py:69
  1174.3 5.1 collective-permute-start
  1504.3 245.4 %all-gather.6.cloned.1.call-start = ((), (), s32[]{:S(2)}) async-start(), calls=%async_computation.2 | async-start | bytes 2662400 | tf_op jit(solution)/shard_map/while/body/eval_jaxpr/all_gather | solution.py:79
  1640.3 5.2 copy-start.2
  1640.3 5.2 copy-start.3
  1640.3 5.2 copy-start.4
  1640.3 5.2 copy-start.5
  1640.3 5.2 copy-start.6
  1640.3 5.2 copy-start.7
  1640.3 5.2 copy-start.8
  1645.4 104.3 %copy-start = (bf16[8192,128]{1,0:T(8,128)(2,1)S(1)}, bf16[8192,128]{1,0:T(8,128)(2,1)}, u32[]{:S(2)}) copy-start(bf16[8192,128]{1,0:T(8,128)(2,1)} %get-tuple-element.572) | copy-start | bytes 6291460 | tf_op jit(solution)/shard_map/while
  1645.7 0.7 copy-start.1
  1753.0 466.7 %all-gather.4.cloned.1.call-start = ((), (), s32[]{:S(2)}) async-start(), calls=%async_computation.1 | async-start | bytes 2662400 | tf_op jit(solution)/shard_map/while/body/eval_jaxpr/all_gather | solution.py:69
  1753.8 5.1 collective-permute-start
  2083.8 245.4 %all-gather.6.cloned.1.call-start = ((), (), s32[]{:S(2)}) async-start(), calls=%async_computation.2 | async-start | bytes 2662400 | tf_op jit(solution)/shard_map/while/body/eval_jaxpr/all_gather | solution.py:79
  2219.7 5.2 copy-start.2
  2219.7 5.2 copy-start.3
  2219.7 5.2 copy-start.4
  2219.7 5.2 copy-start.5
  2219.7 5.2 copy-start.6
  2219.7 5.2 copy-start.7
  2219.7 5.2 copy-start.8
  2224.8 104.3 %copy-start = (bf16[8192,128]{1,0:T(8,128)(2,1)S(1)}, bf16[8192,128]{1,0:T(8,128)(2,1)}, u32[]{:S(2)}) copy-start(bf16[8192,128]{1,0:T(8,128)(2,1)} %get-tuple-element.572) | copy-start | bytes 6291460 | tf_op jit(solution)/shard_map/while
  2225.1 0.7 copy-start.1
  2332.4 466.8 %all-gather.4.cloned.1.call-start = ((), (), s32[]{:S(2)}) async-start(), calls=%async_computation.1 | async-start | bytes 2662400 | tf_op jit(solution)/shard_map/while/body/eval_jaxpr/all_gather | solution.py:69
  2333.2 5.1 collective-permute-start
  2663.2 245.4 %all-gather.6.cloned.1.call-start = ((), (), s32[]{:S(2)}) async-start(), calls=%async_computation.2 | async-start | bytes 2662400 | tf_op jit(solution)/shard_map/while/body/eval_jaxpr/all_gather | solution.py:79
  2799.1 5.2 copy-start.2
  2799.1 5.2 copy-start.3
  2799.1 5.2 copy-start.4
  2799.1 5.2 copy-start.5
  2799.1 5.2 copy-start.6
  2799.2 5.2 copy-start.7
  2799.2 5.2 copy-start.8
  2804.3 104.3 %copy-start = (bf16[8192,128]{1,0:T(8,128)(2,1)S(1)}, bf16[8192,128]{1,0:T(8,128)(2,1)}, u32[]{:S(2)}) copy-start(bf16[8192,128]{1,0:T(8,128)(2,1)} %get-tuple-element.572) | copy-start | bytes 6291460 | tf_op jit(solution)/shard_map/while
  2804.6 0.7 copy-start.1
  2911.8 42.3 %all-reduce.7.cloned.1.call-start = ((), (), s32[]{:S(2)}) async-start(), calls=%async_computation | async-start | bytes 163840 | tf_op jit(solution)/shard_map/psum | solution.py:18
Sparse Core Ops, SparseCore 0:
  346.5 134.8 all-gather.3
  495.4 95.4 all-gather.5
  925.0 135.7 all-gather.3
  1074.7 95.5 all-gather.5
  1504.5 135.7 all-gather.3
  1654.2 95.5 all-gather.5
  2083.9 135.7 all-gather.3
  2233.6 95.4 all-gather.5
  2663.3 135.7 all-gather.3
  2813.1 95.5 all-gather.5
Sparse Core Ops, SparseCore 1:
  2914.9 39.2 all-reduce.6
